TPU v7x, 256 devices: a whole 4x4x8 slice. The times are simulated.
256 devices in a mesh: site: 128 (over z, y, x_hi, core), sector: 2 (over x_lo).
Axes of the slice: x: 4 (x_hi: 2, x_lo: 2; x = x_hi * 2 + x_lo), y: 4, z: 8, core: 2. Of those that a mesh axis runs over, the one named last changes fastest.
Arguments:
- left_env: bfloat16 [128, 2, 30, 128, 128], P('site', 'sector'), may hold values from -6 to 6
- right_env: bfloat16 [128, 2, 30, 128, 128], P('site', 'sector'), may hold values from -6 to 6
- left_site: bfloat16 [128, 2, 4, 128, 128], P('site', 'sector'), may hold values from -0.5 to 0.5
- right_site: bfloat16 [128, 2, 4, 128, 128], P('site', 'sector'), may hold values from -0.5 to 0.5
- left_ket: int32 [128, 2, 30], P('site'), may hold values from 0 to 1
- right_ket: int32 [128, 2, 30], P('site'), may hold values from 0 to 1
- left_terms: int32 [128, 3, 2, 30, 16], P('site'), may hold values from 0 to 59, as said below
- right_terms: int32 [128, 3, 2, 30, 16], P('site'), may hold values from 0 to 59, as said below
- left_weight: float32 [128, 2, 30, 16], P('site'), may hold values from -2 to 2
- right_weight: float32 [128, 2, 30, 16], P('site'), may hold values from -2 to 2
- left_sizes: int32 [128, 2], P('site'), may hold values from 64 to 128
- right_sizes: int32 [128, 2], P('site'), may hold values from 64 to 128
Outputs:
- new_left: bfloat16 [128, 2, 30, 128, 128], P('site', 'sector')
- new_right: bfloat16 [128, 2, 30, 128, 128], P('site', 'sector')
Inputs may be any that keep to these rules, and one draw needn't show every extreme that they name: `left_terms`: field 0 is an environment block index c * 30 + v; in term f of every output block, sector block c lies in owner f // (16 / 2), owners holding 1 block each. Field 1 is a local state below 4; field 2 a site block index a * 4 + s. `right_terms`: as for left_terms.
All inputs are finite; a program needn't handle non-finite values.
Results may differ from a plain program's by a relative error of at most 0.014.
Values may be sent and summed in bfloat16 or wider, within the bound.
A program may use at most 128 MiB of HBM per device.

v0:
```python
import jax
import jax.numpy as jnp
from jax import lax
from jax.sharding import PartitionSpec as P


def shifted(value, axis, steps):
    count = lax.axis_size(axis)
    first, last = (max(0, -steps), min(count, count - steps))
    return lax.ppermute(value, axis, [(source, source + steps) for source in range(first, last)])


def masked_blocks(site_all, sizes):
    width = site_all.shape[-1]
    row_mask = jnp.arange(width)[None, None, :, None] < sizes[:, None, None, None]
    return jnp.where(row_mask, site_all, jnp.zeros_like(site_all))


def half_table(flat_env, blocks, ket_index):
    width = blocks.shape[-1]
    ket_take = blocks[ket_index]
    table = jnp.einsum("npq,nsqr->nspr", flat_env, ket_take, preferred_element_type=jnp.float32)
    return table.astype(jnp.bfloat16).reshape(-1, width, width)


def contract(table, flat_blocks, term_rows, term_weight, bases, degree):
    width = flat_blocks.shape[-1]
    group_count = bases.shape[0]
    segment = table.shape[0] // group_count
    table_groups = table.reshape(group_count, segment, width * width)
    bra_count = flat_blocks.shape[0]
    bra_matrix = flat_blocks.reshape(bra_count, width * width)
    env_cols = jnp.swapaxes(term_rows[0], 0, 1)
    phys_cols = jnp.swapaxes(term_rows[1], 0, 1)
    bra_cols = jnp.swapaxes(term_rows[2], 0, 1)
    weight_cols = jnp.swapaxes(term_weight, 0, 1)

    def one_column(item):
        env_index, physical, bra_index, weights = item
        row_count, term_count = env_index.shape
        per_group = term_count // group_count
        grouped_env = env_index.reshape(row_count, group_count, per_group)
        grouped_phys = physical.reshape(row_count, group_count, per_group)
        local_entry = (grouped_env - bases[None, :, None]) * degree + grouped_phys
        entry_pick = (local_entry[..., None] == jnp.arange(segment)[None, None, None, :]).astype(
            jnp.bfloat16
        )
        half_product = jnp.einsum(
            "rgfl,glx->rgfx", entry_pick, table_groups, preferred_element_type=jnp.float32
        )
        half_product = half_product.astype(jnp.bfloat16).reshape(
            row_count, term_count, width, width
        )
        bra_pick = (bra_index[..., None] == jnp.arange(bra_count)[None, None, :]).astype(
            jnp.bfloat16
        )
        bra_take = jnp.einsum(
            "rfk,kx->rfx", bra_pick, bra_matrix, preferred_element_type=jnp.float32
        )
        bra_take = bra_take.astype(jnp.bfloat16).reshape(row_count, term_count, width, width)
        contribution = jnp.einsum(
            "rfqp,rfqs->rfps", bra_take, half_product, preferred_element_type=jnp.float32
        )
        return jnp.einsum("rf,rfps->rps", weights, contribution)

    result = lax.map(one_column, (env_cols, phys_cols, bra_cols, weight_cols))
    return jnp.swapaxes(result, 0, 1)


def on_device(
    left_env,
    right_env,
    left_site,
    right_site,
    left_ket,
    right_ket,
    left_terms,
    right_terms,
    left_weight,
    right_weight,
    left_sizes,
    right_sizes,
):
    blk_count = left_env.shape[1]
    columns = left_env.shape[2]
    width = left_env.shape[3]
    degree = left_site.shape[2]
    owners = lax.axis_size("sector")
    left_all, right_all = (
        lax.all_gather(left_site, "sector", axis=1, tiled=True),
        lax.all_gather(right_site, "sector", axis=1, tiled=True),
    )
    left_blocks = masked_blocks(left_all[0], left_sizes[0])
    right_blocks = masked_blocks(right_all[0], right_sizes[0])
    left_flat_blocks = left_blocks.reshape(-1, width, width)
    right_flat_blocks = right_blocks.reshape(-1, width, width)
    left_kets = left_ket[0].reshape(-1)
    right_kets = right_ket[0].reshape(-1)
    owner = lax.axis_index("sector")
    left_full, right_full = (
        lax.all_gather(left_env, "sector", axis=1, tiled=True),
        lax.all_gather(right_env, "sector", axis=1, tiled=True),
    )
    first_row = owner * blk_count
    bases = jnp.arange(owners) * blk_count * columns
    left_half = half_table(left_full[0].reshape(-1, width, width), left_blocks, left_kets)
    right_half = half_table(right_full[0].reshape(-1, width, width), right_blocks, right_kets)
    left_table = lax.dynamic_slice_in_dim(left_terms[0], first_row, blk_count, 1)
    right_table = lax.dynamic_slice_in_dim(right_terms[0], first_row, blk_count, 1)
    left_coef = lax.dynamic_slice_in_dim(left_weight[0], first_row, blk_count, 0)
    right_coef = lax.dynamic_slice_in_dim(right_weight[0], first_row, blk_count, 0)
    left_update = contract(left_half, left_flat_blocks, left_table, left_coef, bases, degree)
    right_update = contract(right_half, right_flat_blocks, right_table, right_coef, bases, degree)
    left_ready = left_update.astype(jnp.bfloat16)[None]
    right_ready = right_update.astype(jnp.bfloat16)[None]
    left_received = shifted(left_ready, "site", 1)
    right_received = shifted(right_ready, "site", -1)
    group_index = lax.axis_index("site")
    new_left = jnp.where(group_index == 0, left_env, left_received)
    new_right = jnp.where(group_index == lax.axis_size("site") - 1, right_env, right_received)
    return (new_left, new_right)


def solution(mesh):
    return jax.shard_map(
        on_device,
        mesh=mesh,
        in_specs=(
            P("site", "sector", None, None, None),
            P("site", "sector", None, None, None),
            P("site", "sector", None, None, None),
            P("site", "sector", None, None, None),
            P("site", None, None),
            P("site", None, None),
            P("site", None, None, None, None),
            P("site", None, None, None, None),
            P("site", None, None, None),
            P("site", None, None, None),
            P("site", None),
            P("site", None),
        ),
        out_specs=(P("site", "sector", None, None, None), P("site", "sector", None, None, None)),
        check_vma=False,
    )
```

profile of v0, /device:TPU:1, one launch (start us, length us, event | category | flops | bytes accessed | tf_op | source)
XLA Modules:
  0.0 514.7 jit_solution(15430397051243894927)
XLA Ops:
  10.5 5.3 %all_gather.14 = bf16[1,2,4,128,128]{4,3,2,0,1:T(8,128)(2,1)S(1)} all-gather(bf16[1,1,4,128,128]{4,3,2,0,1:T(8,128)(2,1)} %bitcast.188), channel_id=1, replica_groups=mesh['site'=128,'sector'=2] {'sector'}, dimensions={1}, use_global_device_ids=true | all-gather | bytes 393216 | tf_op jit(solution)/shard_map/all_gather | solution.py:91
  17.7 4.7 all_gather.12
  24.0 5.3 %gather_fusion.1 = bf16[60,4,128,128]{3,2,1,0:T(8,128)(2,1)} fusion(bf16[2,4,128,128]{3,2,1,0:T(8,128)(2,1)S(1)} %bitcast_select_fusion.2, s32[1024]{0:T(1024)S(1)} %pad_clamp_fusion), kind=kCustom, calls=%fused_computation.1 | custom fusion | bytes 15728880 | tf_op jit(solution)/shard_map/gather | solution.py:21
  29.9 5.2 %gather_fusion = bf16[60,4,128,128]{3,2,1,0:T(8,128)(2,1)} fusion(bf16[2,4,128,128]{3,2,1,0:T(8,128)(2,1)S(1)} %bitcast_select_fusion.3, s32[1024]{0:T(1024)S(1)} %pad_clamp_fusion.1), kind=kCustom, calls=%fused_computation | custom fusion | bytes 15728880 | tf_op jit(solution)/shard_map/gather | solution.py:21
  35.5 14.9 %all-gather.5.cloned.1.call-done = bf16[1,2,30,128,128]{4,3,2,0,1:T(8,128)(2,1)} async-done(((bf16[1,1,30,128,128]{4,3,2,0,1:T(8,128)(2,1)}), bf16[1,2,30,128,128]{4,3,2,0,1:T(8,128)(2,1)}) %all-gather.5.cloned.1.call-update) | async-done | bytes 1966096 | tf_op jit(solution)/shard_map/all_gather | solution.py:102
  50.4 9.2 %convert_bitcast_fusion = bf16[60,4,128,128]{2,3,1,0:T(8,128)(2,1)} fusion(bf16[60,4,128,128]{3,2,1,0:T(8,128)(2,1)} %gather_fusion.1, bf16[60,128,128,1]{2,1,3,0:T(8,128)(2,1)} %bitcast.185), kind=kOutput, calls=%fused_computation.46 | convolution fusion | flops 1010565120 | bytes 17694720 | tf_op jit(solution)/shard_map/npq,nsqr->nspr/dot_general | solution.py:22
  59.5 10.7 %copy.46 = bf16[60,4,128,128]{3,2,1,0:T(8,128)(2,1)} copy(bf16[60,4,128,128]{2,3,1,0:T(8,128)(2,1)} %convert_bitcast_fusion) | data formatting | bytes 15728640 | tf_op jit(solution)/shard_map/convert_element_type | solution.py:23
  70.2 12.7 %reshape_reshape.9 = bf16[2,120,16384]{2,1,0:T(8,128)(2,1)} reshape(bf16[60,4,128,128]{3,2,1,0:T(8,128)(2,1)} %copy.46) | data formatting | bytes 15728640 | tf_op jit(solution)/shard_map/reshape;reshape | solution.py:30
  83.2 185.1 %while.23 = (s32[]{:T(128)}, bf16[30,1,128,128]{3,2,1,0:T(8,128)(2,1)S(1)}, bf16[30,1,16]{2,1,0:T(2,128)(2,1)S(1)}, s32[30,1,16]{2,1,0:T(1,128)S(1)}, bf16[8,163...) while((s32[]{:T(128)}, ...), condition=%wide.region_3.4_spmd.clone, body=%wide.region_2.3_spmd.clone.sunk | while | flops 135268400 | bytes 13567549 | solution.py:66
  89.6 4.5 fusion.89
  132.8 4.5 fusion.89
  145.1 4.5 fusion.89
  157.5 4.5 fusion.89
  176.0 4.5 fusion.89
  188.3 4.5 fusion.89
  213.0 4.5 fusion.89
  231.5 4.5 fusion.89
  243.8 4.5 fusion.89
  272.1 9.2 %convert_bitcast_fusion.1 = bf16[60,4,128,128]{2,3,1,0:T(8,128)(2,1)} fusion(bf16[60,4,128,128]{3,2,1,0:T(8,128)(2,1)} %gather_fusion, bf16[60,128,128,1]{2,1,3,0:T(8,128)(2,1)} %bitcast.184), kind=kOutput, calls=%fused_computation.47 | convolution fusion | flops 1010565120 | bytes 17694720 | tf_op jit(solution)/shard_map/npq,nsqr->nspr/dot_general | solution.py:22
  281.3 10.6 %copy.39 = bf16[60,4,128,128]{3,2,1,0:T(8,128)(2,1)} copy(bf16[60,4,128,128]{2,3,1,0:T(8,128)(2,1)} %convert_bitcast_fusion.1) | data formatting | bytes 15728640 | tf_op jit(solution)/shard_map/convert_element_type | solution.py:23
  291.9 12.6 %reshape_reshape.8 = bf16[2,120,16384]{2,1,0:T(8,128)(2,1)} reshape(bf16[60,4,128,128]{3,2,1,0:T(8,128)(2,1)} %copy.39) | data formatting | bytes 15728640 | tf_op jit(solution)/shard_map/reshape;reshape | solution.py:30
  304.8 185.2 %while.22 = (s32[]{:T(128)}, bf16[30,1,128,128]{3,2,1,0:T(8,128)(2,1)S(1)}, bf16[30,1,16]{2,1,0:T(2,128)(2,1)S(1)}, s32[30,1,16]{2,1,0:T(1,128)S(1)}, bf16[8,163...) while((s32[]{:T(128)}, ...), condition=%wide.region_1.2_spmd.clone, body=%wide.region_0.1_spmd.clone.sunk | while | flops 135268400 | bytes 13567549 | solution.py:66
  305.1 4.7 fusion.77
  497.8 9.1 %collective-permute-done = bf16[1,1,30,128,128]{4,3,2,1,0:T(8,128)(2,1)S(1)} collective-permute-done((bf16[1,1,30,128,128]{4,3,2,1,0:T(8,128)(2,1)}, bf16[1,1,30,128,128]{4,3,2,1,0:T(8,128)(2,1)S(1)}, u32[]{:S(2)}, u32[]{:S(2)}) %collective-permute-start) | collective-permute-done | bytes 983072 | tf_op jit(solution)/shard_map/ppermute | solution.py:10
  (812 shorter events, 341.9 us)
Async XLA Ops:
  7.2 43.2 %all-gather.5.cloned.1.call-start = ((), (), s32[]{:S(2)}) async-start(), calls=%async_computation.1 | async-start | bytes 2949120 | tf_op jit(solution)/shard_map/all_gather | solution.py:102
  7.9 264.1 %all-gather.3.cloned.1.call-start = ((), (), s32[]{:S(2)}) async-start(), calls=%async_computation | async-start | bytes 2949120 | tf_op jit(solution)/shard_map/all_gather | solution.py:101
  269.2 226.2 %collective-permute-start.1 = (bf16[1,1,30,128,128]{4,3,2,1,0:T(8,128)(2,1)}, bf16[1,1,30,128,128]{4,3,2,1,0:T(8,128)(2,1)}, u32[]{:S(2)}, u32[]{:S(2)}) collective-permute-start(bf16[1,1,30,128,128]{4,3,2,1,0:T(8,128)(2,1)} %fusion.27), channel_id=1, source_target_pairs={{2,0},{4,2},{6,4},{8,6},{10,8},{12,10},{14,12},{16,14},{18,16},{20... | collective-permute-start | bytes 2949128 | tf_op jit(solution)/shard_map/ppermute | solution.py:10
  304.8 190.7 %copy-start = (bf16[1,1,30,128,128]{4,3,2,1,0:T(8,128)(2,1)S(1)}, bf16[1,1,30,128,128]{4,3,2,1,0:T(8,128)(2,1)}, u32[]{:S(2)}) copy-start(bf16[1,1,30,128,128]{4,3,2,1,0:T(8,128)(2,1)} %param.17) | copy-start | bytes 2949124
  304.8 202.0 %copy-start.1 = (bf16[1,1,30,128,128]{4,3,2,1,0:T(8,128)(2,1)S(1)}, bf16[1,1,30,128,128]{4,3,2,1,0:T(8,128)(2,1)}, u32[]{:S(2)}) copy-start(bf16[1,1,30,128,128]{4,3,2,1,0:T(8,128)(2,1)} %param.16) | copy-start | bytes 2949124
  491.0 15.8 %collective-permute-start = (bf16[1,1,30,128,128]{4,3,2,1,0:T(8,128)(2,1)}, bf16[1,1,30,128,128]{4,3,2,1,0:T(8,128)(2,1)S(1)}, u32[]{:S(2)}, u32[]{:S(2)}) collective-permute-start(bf16[1,1,30,128,128]{4,3,2,1,0:T(8,128)(2,1)} %fusion.26), channel_id=1, source_target_pairs={{0,2},{2,4},{4,6},{6,8},{8,10},{10,12},{12,14},{14,16},{16,18},{18... | collective-permute-start | bytes 2949128 | tf_op jit(solution)/shard_map/ppermute | solution.py:10
Sparse Core Ops, SparseCore 0:
  9.8 40.5 all-gather.4
  52.1 37.6 all-gather.2
where the time goes:
time: 525 us; the launch traced here: 515 us
  matrix products  356 us (68%)
  local copies, waits for them, and re-layouts  88 us (17%)
  waiting for transfers between devices  25.3 us (5%)
  between operations  14.2 us (3%)
  other arithmetic  10.3 us (2%)
  blocking collectives  10 us (2%)
  starting transfers between devices  7.3 us (1%)
    dot_general x60, matrix products, one_column(): jnp.einsum('rgfl,glx->rgfx', entry_pick, table_groups, preferred_element_...  272 us
    another operation x2, local copies, waits for them, and re-layouts, contract(): table_groups = table.reshape(group_count, segment, width * width)  25.3 us
    dot_general x60, matrix products, one_column(): return jnp.einsum('rf,rfps->rps', weights, contribution)  23.7 us
    convert_element_type x2, local copies, waits for them, and re-layouts, half_table(): return table.astype(jnp.bfloat16).reshape(-1, width, width)  21.4 us
    dot_general x60, matrix products, one_column(): jnp.einsum('rfqp,rfqs->rfps', bra_take, half_product, preferred_element_t...  21 us
    dot_general x60, matrix products, one_column(): jnp.einsum('rfk,kx->rfx', bra_pick, bra_matrix, preferred_element_type=jn...  20.6 us
    dot_general x2, matrix products, half_table(): jnp.einsum('npq,nsqr->nspr', flat_env, ket_take, preferred_element_type=j...  18.4 us
    all_gather x1, waiting for transfers between devices, on_device(): lax.all_gather(right_env, 'sector', axis=1, tiled=True)  14.9 us
  transfers between devices with their start and end apart: 4, of which 2 were waited for; matrix products, arithmetic and copies ran while one was open for 88% of the time, Pallas kernels for 0%

commit v1 on v0

v1 whole, which is shorter than its diff:
```python
import functools

import jax
import jax.numpy as jnp
from jax import lax
from jax.experimental import pallas as pl
from jax.experimental.pallas import tpu as pltpu
from jax.sharding import PartitionSpec as P

MESH = pl.DeviceIdType.MESH
CHUNK = 2
HALF_STEP = 2


def kernel(
    sites,
    left_env,
    right_env,
    left_site,
    right_site,
    left_ket,
    right_ket,
    left_terms,
    right_terms,
    left_weight,
    right_weight,
    left_sizes,
    right_sizes,
    out,
    env,
    site,
    ket,
    terms,
    weight,
    sizes,
    joined,
    bra,
    half,
    send,
    keep,
    recv,
    final,
    load_sem,
    site_send_sem,
    site_recv_sem,
    part_send_sem,
    part_recv_sem,
    out_send_sem,
    out_recv_sem,
    edge_sem,
):
    columns, width = env.shape[1], env.shape[2]
    degree = site.shape[2]
    term_count = terms.shape[3] // 2
    chunks = columns // CHUNK
    g, c = lax.axis_index("site"), lax.axis_index("sector")
    core = lax.rem(g, 2)
    other = 1 - c
    edge = (g == 0) | (g == sites - 1)
    mate = g + 1 - 2 * core
    far = lax.rem(g + 2 * core - 1 + sites, sites)

    loads = []
    for side, refs in enumerate(
        (
            (left_site, left_env, left_sizes, left_ket, left_terms, left_weight),
            (right_site, right_env, right_sizes, right_ket, right_terms, right_weight),
        )
    ):
        site_in, env_in, sizes_in, ket_in, terms_in, weight_in = refs
        for source, target in (
            (site_in.at[0, 0], site.at[side, c]),
            (env_in.at[0, 0], env.at[side]),
            (sizes_in.at[0], sizes.at[side]),
            (ket_in.at[0], ket.at[side]),
            (terms_in.at[0], terms.at[side]),
            (weight_in.at[0], weight.at[side]),
        ):
            loads.append(pltpu.make_async_copy(source, target, load_sem.at[len(loads)]))
    for load in loads:
        load.start()

    barrier = pltpu.get_barrier_semaphore()
    for peer in ((g, other), (mate, c), (far, other)):
        pl.semaphore_signal(barrier, inc=1, device_id=peer, device_id_type=MESH)
    pl.semaphore_wait(barrier, 3)
    per_side = len(loads) // 2
    loads[0].wait()
    loads[per_side].wait()

    def side_of(phase):
        return 1 - core if phase == 0 else core

    def site_copy(side, owner):
        return pltpu.make_async_remote_copy(
            src_ref=site.at[side, owner],
            dst_ref=site.at[side, owner],
            send_sem=site_send_sem.at[side],
            recv_sem=site_recv_sem.at[side],
            device_id=(g, other),
            device_id_type=MESH,
        )

    def part_copy(phase, chunk):
        blocks = pl.ds(chunk * CHUNK, CHUNK)
        return pltpu.make_async_remote_copy(
            src_ref=send.at[phase, blocks],
            dst_ref=recv.at[phase, blocks],
            send_sem=part_send_sem.at[phase, chunk],
            recv_sem=part_recv_sem.at[phase, chunk],
            device_id=(g, other),
            device_id_type=MESH,
        )

    def out_copy(phase, chunk, out_side):
        blocks = pl.ds(chunk * CHUNK, CHUNK)
        return pltpu.make_async_remote_copy(
            src_ref=final.at[phase, blocks],
            dst_ref=out.at[out_side, blocks],
            send_sem=out_send_sem.at[phase, chunk],
            recv_sem=out_recv_sem.at[phase, chunk],
            device_id=(far, other) if phase == 0 else (mate, c),
            device_id_type=MESH,
        )

    for phase in range(2):
        site_copy(side_of(phase), c).start()
    for side in range(2):
        for load in loads[side * per_side + 1 : (side + 1) * per_side]:
            load.wait()
    edge_copy = pltpu.make_async_copy(env.at[core], out.at[core], edge_sem)

    @pl.when(edge)
    def _():
        edge_copy.start()

    def prepare(side):
        site_copy(side, other).wait_recv()
        row = lax.broadcasted_iota(jnp.int32, (width, width), 0)

        def one(a, carry):
            inside = row < sizes[side, a]
            for s in range(degree):
                block = jnp.where(inside, site[side, a, s].astype(jnp.float32), 0.0)
                joined[side, a, :, s * width : (s + 1) * width] = block.astype(jnp.bfloat16)
                bra[side, a * degree + s] = block.T
            return carry

        lax.fori_loop(0, 2, one, 0)

        def step(i, carry):
            rows = []
            for b in range(HALF_STEP):
                v = i * HALF_STEP + b
                block = env[side, v]
                second = ket[side, c, v].astype(jnp.float32).astype(jnp.bfloat16)
                first = (1 - ket[side, c, v]).astype(jnp.float32).astype(jnp.bfloat16)
                rows.append(jnp.concatenate([block * first, block * second], axis=1))
            both = jnp.concatenate([joined[side, 0], joined[side, 1]], axis=0)
            table = jnp.dot(
                jnp.concatenate(rows, axis=0), both, preferred_element_type=jnp.float32
            ).astype(jnp.bfloat16)
            for b in range(HALF_STEP):
                for t in range(degree):
                    half[side, (i * HALF_STEP + b) * degree + t] = table[
                        b * width : (b + 1) * width, t * width : (t + 1) * width
                    ]
            return carry

        lax.fori_loop(0, columns // HALF_STEP, step, 0)

    def partial_sum(side, k, w):
        bras, halves = [], []
        for j in range(term_count):
            f = c * term_count + j
            v = jnp.maximum(terms[side, 0, k, f, w] - c * columns, 0)
            t = terms[side, 1, k, f, w]
            u = terms[side, 2, k, f, w]
            bras.append((bra[side, u] * weight[side, k, f, w]).astype(jnp.bfloat16))
            halves.append(half[side, v * degree + t])
        return jnp.dot(
            jnp.concatenate(bras, axis=1),
            jnp.concatenate(halves, axis=0),
            preferred_element_type=jnp.float32,
        )

    for phase in range(2):
        side = side_of(phase)
        prepare(side)
        sent_sector = c if phase == 0 else other

        def send_step(chunk, carry):
            for b in range(CHUNK):
                w = chunk * CHUNK + b
                send[phase, w] = partial_sum(side, sent_sector, w).astype(jnp.bfloat16)
            part_copy(phase, chunk).start()
            return carry

        lax.fori_loop(0, chunks, send_step, 0)

    for phase in range(2):
        side = side_of(phase)
        kept_sector = other if phase == 0 else c

        def keep_step(w, carry):
            keep[phase, w] = partial_sum(side, kept_sector, w)
            return carry

        lax.fori_loop(0, columns, keep_step, 0)

        def add_step(chunk, carry):
            part_copy(phase, chunk).wait_recv()
            for b in range(CHUNK):
                w = chunk * CHUNK + b
                total = keep[phase, w] + recv[phase, w].astype(jnp.float32)
                final[phase, w] = total.astype(jnp.bfloat16)
            copy = out_copy(phase, chunk, side)
            if phase == 0:

                @pl.when(jnp.logical_not(edge))
                def _():
                    copy.start()

            else:
                copy.start()
            return carry

        lax.fori_loop(0, chunks, add_step, 0)

    for phase in range(2):
        site_copy(side_of(phase), c).wait_send()

        def drain_step(chunk, carry):
            part_copy(phase, chunk).wait_send()
            copy = out_copy(phase, chunk, 1 - side_of(phase))
            if phase == 0:

                @pl.when(jnp.logical_not(edge))
                def _():
                    copy.wait()

            else:
                copy.wait()
            return carry

        lax.fori_loop(0, chunks, drain_step, 0)

    @pl.when(edge)
    def _():
        edge_copy.wait()


def on_device(*args):
    args = args[:6] + tuple(jnp.swapaxes(table, -1, -2) for table in args[6:10]) + args[10:]
    left_env, left_site, left_ket, left_terms = args[0], args[2], args[4], args[6]
    columns, width = left_env.shape[2], left_env.shape[3]
    degree = left_site.shape[2]
    chunks = columns // CHUNK
    blocks = (columns, width, width)
    bf16, f32 = jnp.bfloat16, jnp.float32
    sites = lax.axis_size("site")
    out = pl.pallas_call(
        functools.partial(kernel, sites),
        out_shape=jax.ShapeDtypeStruct((2,) + blocks, bf16),
        in_specs=[pl.BlockSpec(memory_space=pl.ANY)] * len(args),
        out_specs=pl.BlockSpec(memory_space=pl.ANY),
        scratch_shapes=[
            pltpu.VMEM((2,) + blocks, bf16),
            pltpu.VMEM((2, 2, degree, width, width), bf16),
            pltpu.SMEM((2,) + left_ket.shape[1:], jnp.int32),
            pltpu.SMEM((2,) + left_terms.shape[1:], jnp.int32),
            pltpu.SMEM((2,) + left_terms.shape[2:], f32),
            pltpu.SMEM((2, 2), jnp.int32),
            pltpu.VMEM((2, 2, width, degree * width), bf16),
            pltpu.VMEM((2, 2 * degree, width, width), f32),
            pltpu.VMEM((2, columns * degree, width, width), bf16),
            pltpu.VMEM((2,) + blocks, bf16),
            pltpu.VMEM((2,) + blocks, f32),
            pltpu.VMEM((2,) + blocks, bf16),
            pltpu.VMEM((2,) + blocks, bf16),
            pltpu.SemaphoreType.DMA((len(args),)),
            pltpu.SemaphoreType.DMA((2,)),
            pltpu.SemaphoreType.DMA((2,)),
            pltpu.SemaphoreType.DMA((2, chunks)),
            pltpu.SemaphoreType.DMA((2, chunks)),
            pltpu.SemaphoreType.DMA((2, chunks)),
            pltpu.SemaphoreType.DMA((2, chunks)),
            pltpu.SemaphoreType.DMA,
        ],
        compiler_params=pltpu.CompilerParams(
            collective_id=0, has_side_effects=True, vmem_limit_bytes=40 * 1024 * 1024
        ),
    )(*args)
    return out[0][None, None], out[1][None, None]


def solution(mesh):
    blocks = P("site", "sector", None, None, None)
    return jax.shard_map(
        on_device,
        mesh=mesh,
        in_specs=(
            blocks,
            blocks,
            blocks,
            blocks,
            P("site", None, None),
            P("site", None, None),
            P("site", None, None, None, None),
            P("site", None, None, None, None),
            P("site", None, None, None),
            P("site", None, None, None),
            P("site", None),
            P("site", None),
        ),
        out_specs=(blocks, blocks),
        check_vma=False,
    )
```

time: 525 us -> 73.5 us (0.14); the launches traced: 515 us -> 73 us
  matrix products: 356 us -> 0 us
  local copies, waits for them, and re-layouts: 88 us -> 11.3 us
  Pallas kernels: 0 us -> 61.1 us
  waiting for transfers between devices: 25.3 us -> 0 us
  between operations: 14.2 us -> 0.66 us
  other arithmetic: 10.3 us -> 0 us
  blocking collectives: 10 us -> 0 us
  starting transfers between devices: 7.3 us -> 0 us
    dot_general x242 -> x0, matrix products: 356 us -> none  [the longest x60 272 us: one_column(): jnp.einsum('rgfl,glx->rgfx', entry_pick, table_groups, preferred_element_...]
    pallas_call x0 -> x1, Pallas kernels: none -> 61.1 us  [on_device(): pl.pallas_call(functools.partial(kernel, sites), out_shape=jax.ShapeDtype...]
    another operation x6 -> x1, local copies, waits for them, and re-layouts: 27.3 us -> 1.4 us  [on_device(): return (out[0][None, None], out[1][None, None])]
    convert_element_type x4 -> x0, local copies, waits for them, and re-layouts: 23.4 us -> none  [the longest x2 21.4 us: half_table(): return table.astype(jnp.bfloat16).reshape(-1, width, width)]
    all_gather x2 -> x0, waiting for transfers between devices: 14.9 us -> none  [the longest x1 14.9 us: on_device(): lax.all_gather(right_env, 'sector', axis=1, tiled=True)]
    while x120 -> x0, local copies, waits for them, and re-layouts: 11.8 us -> none
    gather x2 -> x0, local copies, waits for them, and re-layouts: 10.5 us -> none  [half_table(): ket_take = blocks[ket_index]]
    all_gather x2 -> x0, blocking collectives: 10 us -> none  [the longest x1 5.32 us: on_device(): lax.all_gather(right_site, 'sector', axis=1, tiled=True)]
  transfers between devices with their start and end apart: 4 -> 0, of which waited for: 2 -> 0; matrix products, arithmetic and copies ran while one was open for 88% -> 0% of each run, Pallas kernels for 0% -> 0%
where the time goes in v1:
time: 73.5 us; the launch traced here: 73 us
  Pallas kernels  61.1 us (83%)
  local copies, waits for them, and re-layouts  11.3 us (15%)
    pallas_call x1, Pallas kernels, on_device(): pl.pallas_call(functools.partial(kernel, sites), out_shape=jax.ShapeDtype...  61.1 us
    unnamed x24, local copies, waits for them, and re-layouts  9.9 us

profile of v1, /device:TPU:1, one launch (start us, length us, event | category | flops | bytes accessed | tf_op | source)
XLA Modules:
  0.0 73.0 jit_solution(1318969987027616091)
XLA Ops:
  0.6 0.0 copy-start
  0.6 1.2 %copy-done = bf16[1,1,30,128,128]{4,3,2,1,0:T(8,128)(2,1)S(1)} copy-done((bf16[1,1,30,128,128]{4,3,2,1,0:T(8,128)(2,1)S(1)}, bf16[1,1,30,128,128]{4,3,2,1,0:T(8,128)(2,1)}, u32[]{:S(2)}) %copy-start) | copy-done | bytes 983064
  1.8 0.0 copy-start.1
  1.8 1.2 %copy-done.1 = bf16[1,1,30,128,128]{4,3,2,1,0:T(8,128)(2,1)S(1)} copy-done((bf16[1,1,30,128,128]{4,3,2,1,0:T(8,128)(2,1)S(1)}, bf16[1,1,30,128,128]{4,3,2,1,0:T(8,128)(2,1)}, u32[]{:S(2)}) %copy-start.1) | copy-done | bytes 983064
  3.0 0.0 copy-start.2
  3.0 0.9 %copy-done.2 = bf16[1,1,4,128,128]{4,3,2,1,0:T(8,128)(2,1)S(1)} copy-done((bf16[1,1,4,128,128]{4,3,2,1,0:T(8,128)(2,1)S(1)}, bf16[1,1,4,128,128]{4,3,2,1,0:T(8,128)(2,1)}, u32[]{:S(2)}) %copy-start.2) | copy-done | bytes 131096
  3.9 0.0 copy-start.3
  3.9 0.9 %copy-done.3 = bf16[1,1,4,128,128]{4,3,2,1,0:T(8,128)(2,1)S(1)} copy-done((bf16[1,1,4,128,128]{4,3,2,1,0:T(8,128)(2,1)S(1)}, bf16[1,1,4,128,128]{4,3,2,1,0:T(8,128)(2,1)}, u32[]{:S(2)}) %copy-start.3) | copy-done | bytes 131096
  4.8 0.0 copy-start.4
  4.9 0.8 %copy-done.4 = s32[1,3,2,30,16]{3,4,2,1,0:T(8,128)S(1)} copy-done((s32[1,3,2,30,16]{3,4,2,1,0:T(8,128)S(1)}, s32[1,3,2,30,16]{3,4,2,1,0:T(8,128)}, u32[]{:S(2)}) %copy-start.4) | copy-done | bytes 11544
  5.6 0.0 copy-start.5
  5.7 0.8 %copy-done.5 = s32[1,3,2,30,16]{3,4,2,1,0:T(8,128)S(1)} copy-done((s32[1,3,2,30,16]{3,4,2,1,0:T(8,128)S(1)}, s32[1,3,2,30,16]{3,4,2,1,0:T(8,128)}, u32[]{:S(2)}) %copy-start.5) | copy-done | bytes 11544
  6.4 0.0 copy-start.6
  6.4 0.7 copy-done.6
  7.2 0.0 copy-start.7
  7.2 0.7 copy-done.7
  7.9 0.0 copy-start.8
  7.9 0.7 copy-done.8
  8.6 0.0 copy-start.9
  8.6 0.7 copy-done.9
  9.2 0.7 copy-done.10
  9.9 0.7 copy-done.11
  10.6 61.1 %shard_map.131 = bf16[2,30,128,128]{3,2,1,0:T(8,128)(2,1)S(1)} custom-call(bf16[1,1,30,128,128]{4,3,2,1,0:T(8,128)(2,1)S(1)} %copy-done, bf16[1,1,30,128,128]{4,3,2,1,0:T(8,128)(2,1)S(1)} %copy-done.1, bf16[1,1,4,128,128]{4,3,2,1,0:T(8,128)(2,1)S(1)} %copy-done.2, bf16[1,1,4,128,128]{4,3,2,1,0:T(8,128)(2,1)S(1)} %copy-done.3, s32[1,2,30]{2,1,0:T(2,128)S(1)} %copy-done.8, ...), custom_call_target="tpu_custom_call" | custom-call | tf_op jit(solution)/shard_map/pallas_call | solution.py:262
  71.6 1.4 %slice_bitcast_fusion = (bf16[1,1,30,128,128]{4,3,2,1,0:T(8,128)(2,1)}, bf16[1,1,30,128,128]{4,3,2,1,0:T(8,128)(2,1)}) fusion(bf16[2,30,128,128]{3,2,1,0:T(8,128)(2,1)S(1)} %shard_map.131), kind=kLoop, calls=%fused_computation | loop fusion | bytes 3932160 | tf_op jit(solution)/shard_map/broadcast_in_dim;squeeze | solution.py:294
  (2 shorter events, 0.0 us)
Async XLA Ops:
  0.6 1.2 %copy-start = (bf16[1,1,30,128,128]{4,3,2,1,0:T(8,128)(2,1)S(1)}, bf16[1,1,30,128,128]{4,3,2,1,0:T(8,128)(2,1)}, u32[]{:S(2)}) copy-start(bf16[1,1,30,128,128]{4,3,2,1,0:T(8,128)(2,1)} %left_env.1) | copy-start | bytes 2949124
  1.8 1.2 %copy-start.1 = (bf16[1,1,30,128,128]{4,3,2,1,0:T(8,128)(2,1)S(1)}, bf16[1,1,30,128,128]{4,3,2,1,0:T(8,128)(2,1)}, u32[]{:S(2)}) copy-start(bf16[1,1,30,128,128]{4,3,2,1,0:T(8,128)(2,1)} %right_env.1) | copy-start | bytes 2949124
  3.0 0.9 %copy-start.2 = (bf16[1,1,4,128,128]{4,3,2,1,0:T(8,128)(2,1)S(1)}, bf16[1,1,4,128,128]{4,3,2,1,0:T(8,128)(2,1)}, u32[]{:S(2)}) copy-start(bf16[1,1,4,128,128]{4,3,2,1,0:T(8,128)(2,1)} %left_site.1) | copy-start | bytes 393220
  3.9 0.9 %copy-start.3 = (bf16[1,1,4,128,128]{4,3,2,1,0:T(8,128)(2,1)S(1)}, bf16[1,1,4,128,128]{4,3,2,1,0:T(8,128)(2,1)}, u32[]{:S(2)}) copy-start(bf16[1,1,4,128,128]{4,3,2,1,0:T(8,128)(2,1)} %right_site.1) | copy-start | bytes 393220
  4.8 0.8 %copy-start.4 = (s32[1,3,2,30,16]{3,4,2,1,0:T(8,128)S(1)}, s32[1,3,2,30,16]{3,4,2,1,0:T(8,128)}, u32[]{:S(2)}) copy-start(s32[1,3,2,30,16]{3,4,2,1,0:T(8,128)} %param.18) | copy-start | bytes 34564
  5.6 0.8 %copy-start.5 = (s32[1,3,2,30,16]{3,4,2,1,0:T(8,128)S(1)}, s32[1,3,2,30,16]{3,4,2,1,0:T(8,128)}, u32[]{:S(2)}) copy-start(s32[1,3,2,30,16]{3,4,2,1,0:T(8,128)} %param.19) | copy-start | bytes 34564
  6.4 0.7 copy-start.6
  7.2 0.7 copy-start.7
  7.9 0.7 copy-start.8
  8.6 0.7 copy-start.9
  9.2 0.7 copy-start.10
  9.9 0.7 copy-start.11

commit v2 on v1

--- a/solution.py
+++ b/solution.py
@@ -262,7 +262,7 @@
     out = pl.pallas_call(
         functools.partial(kernel, sites),
         out_shape=jax.ShapeDtypeStruct((2,) + blocks, bf16),
-        in_specs=[pl.BlockSpec(memory_space=pl.ANY)] * len(args),
+        in_specs=[pl.BlockSpec(memory_space=pltpu.HBM)] * len(args),
         out_specs=pl.BlockSpec(memory_space=pl.ANY),
         scratch_shapes=[
             pltpu.VMEM((2,) + blocks, bf16),
@@ -290,7 +290,7 @@
         compiler_params=pltpu.CompilerParams(
             collective_id=0, has_side_effects=True, vmem_limit_bytes=40 * 1024 * 1024
         ),
-    )(*args)
+    )(*[pltpu.with_memory_space_constraint(a, pltpu.HBM) for a in args])
     return out[0][None, None], out[1][None, None]
 
 

time: 73.5 us -> 62.6 us (0.85)
  local copies, waits for them, and re-layouts: 11.3 us -> 1.5 us
  Pallas kernels: 61.1 us -> 60.3 us
    unnamed x24 -> x0, local copies, waits for them, and re-layouts: 9.9 us -> none
    pallas_call x1, Pallas kernels: 61.1 us -> 60.3 us  [on_device(): pl.pallas_call(functools.partial(kernel, sites), out_shape=jax.ShapeDtype...]
where the time goes in v2:
time: 62.6 us; the launch traced here: 62.5 us
  Pallas kernels  60.3 us (96%)
  local copies, waits for them, and re-layouts  1.5 us (2%)
  between operations  0.64 us (1%)
    pallas_call x1, Pallas kernels, on_device(): pl.pallas_call(functools.partial(kernel, sites), out_shape=jax.ShapeDtype...  60.3 us
    another operation x1, local copies, waits for them, and re-layouts, on_device(): return (out[0][None, None], out[1][None, None])  1.5 us

profile of v2, /device:TPU:1, one launch (start us, length us, event | category | flops | bytes accessed | tf_op | source)
XLA Modules:
  0.0 62.5 jit_solution(6913750259559691500)
XLA Ops:
  0.6 60.3 %shard_map.131 = bf16[2,30,128,128]{3,2,1,0:T(8,128)(2,1)S(1)} custom-call(bf16[1,1,30,128,128]{4,3,2,1,0:T(8,128)(2,1)} %left_env.1, bf16[1,1,30,128,128]{4,3,2,1,0:T(8,128)(2,1)} %right_env.1, bf16[1,1,4,128,128]{4,3,2,1,0:T(8,128)(2,1)} %left_site.1, bf16[1,1,4,128,128]{4,3,2,1,0:T(8,128)(2,1)} %right_site.1, s32[1,2,30]{2,1,0:T(2,128)} %left_ket.1, ...), custom_call_target="tpu_custom_call" | custom-call | tf_op jit(solution)/shard_map/pallas_call | solution.py:262
  61.0 1.5 %slice_bitcast_fusion = (bf16[1,1,30,128,128]{4,3,2,1,0:T(8,128)(2,1)}, bf16[1,1,30,128,128]{4,3,2,1,0:T(8,128)(2,1)}) fusion(bf16[2,30,128,128]{3,2,1,0:T(8,128)(2,1)S(1)} %shard_map.131), kind=kLoop, calls=%fused_computation | loop fusion | bytes 3932160 | tf_op jit(solution)/shard_map/broadcast_in_dim;squeeze | solution.py:294

commit v3 on v2

--- a/solution.py
+++ b/solution.py
@@ -9,7 +9,7 @@
 
 MESH = pl.DeviceIdType.MESH
 CHUNK = 2
-HALF_STEP = 2
+HALF_STEP = 10
 
 
 def kernel(
@@ -39,12 +39,16 @@
     send,
     keep,
     recv,
+    mate_send,
+    mate_recv,
     final,
     load_sem,
     site_send_sem,
     site_recv_sem,
     part_send_sem,
     part_recv_sem,
+    mate_send_sem,
+    mate_recv_sem,
     out_send_sem,
     out_recv_sem,
     edge_sem,
@@ -56,7 +60,8 @@
     g, c = lax.axis_index("site"), lax.axis_index("sector")
     core = lax.rem(g, 2)
     other = 1 - c
-    edge = (g == 0) | (g == sites - 1)
+    inner = (g > 0) & (g < sites - 1)
+    edge = jnp.logical_not(inner)
     mate = g + 1 - 2 * core
     far = lax.rem(g + 2 * core - 1 + sites, sites)
 
@@ -81,9 +86,14 @@
         load.start()
 
     barrier = pltpu.get_barrier_semaphore()
-    for peer in ((g, other), (mate, c), (far, other)):
+    for peer in ((g, other), (mate, c), (mate, other)):
         pl.semaphore_signal(barrier, inc=1, device_id=peer, device_id_type=MESH)
-    pl.semaphore_wait(barrier, 3)
+
+    @pl.when(inner)
+    def _():
+        pl.semaphore_signal(barrier, inc=1, device_id=(far, other), device_id_type=MESH)
+
+    pl.semaphore_wait(barrier, jnp.where(inner, 4, 3))
     per_side = len(loads) // 2
     loads[0].wait()
     loads[per_side].wait()
@@ -101,27 +111,32 @@
             device_id_type=MESH,
         )
 
-    def part_copy(phase, chunk):
+    def chunk_copy(source, target, send_sems, recv_sems, chunk, device):
         blocks = pl.ds(chunk * CHUNK, CHUNK)
         return pltpu.make_async_remote_copy(
-            src_ref=send.at[phase, blocks],
-            dst_ref=recv.at[phase, blocks],
-            send_sem=part_send_sem.at[phase, chunk],
-            recv_sem=part_recv_sem.at[phase, chunk],
-            device_id=(g, other),
+            src_ref=source.at[blocks],
+            dst_ref=target.at[blocks],
+            send_sem=send_sems.at[chunk],
+            recv_sem=recv_sems.at[chunk],
+            device_id=device,
             device_id_type=MESH,
         )
 
-    def out_copy(phase, chunk, out_side):
-        blocks = pl.ds(chunk * CHUNK, CHUNK)
-        return pltpu.make_async_remote_copy(
-            src_ref=final.at[phase, blocks],
-            dst_ref=out.at[out_side, blocks],
-            send_sem=out_send_sem.at[phase, chunk],
-            recv_sem=out_recv_sem.at[phase, chunk],
-            device_id=(far, other) if phase == 0 else (mate, c),
-            device_id_type=MESH,
-        )
+    def part_copy(phase, chunk):
+        return chunk_copy(
+            send.at[phase],
+            recv.at[phase],
+            part_send_sem.at[phase],
+            part_recv_sem.at[phase],
+            chunk,
+            (g if phase == 0 else mate, other),
+        )
+
+    def mate_copy(chunk):
+        return chunk_copy(mate_send, mate_recv, mate_send_sem, mate_recv_sem, chunk, (mate, c))
+
+    def out_copy(chunk, side):
+        return chunk_copy(final, out.at[side], out_send_sem, out_recv_sem, chunk, (far, other))
 
     for phase in range(2):
         site_copy(side_of(phase), c).start()
@@ -134,20 +149,16 @@
     def _():
         edge_copy.start()
 
-    def prepare(side):
-        site_copy(side, other).wait_recv()
-        row = lax.broadcasted_iota(jnp.int32, (width, width), 0)
-
-        def one(a, carry):
-            inside = row < sizes[side, a]
-            for s in range(degree):
-                block = jnp.where(inside, site[side, a, s].astype(jnp.float32), 0.0)
-                joined[side, a, :, s * width : (s + 1) * width] = block.astype(jnp.bfloat16)
-                bra[side, a * degree + s] = block.T
-            return carry
-
-        lax.fori_loop(0, 2, one, 0)
-
+    row = lax.broadcasted_iota(jnp.int32, (width, width), 0)
+
+    def prepare(side, a):
+        inside = row < sizes[side, a]
+        for s in range(degree):
+            block = jnp.where(inside, site[side, a, s].astype(jnp.float32), 0.0)
+            joined[side, a, :, s * width : (s + 1) * width] = block.astype(jnp.bfloat16)
+            bra[side, a * degree + s] = block.T
+
+    def fill_half(side):
         def step(i, carry):
             rows = []
             for b in range(HALF_STEP):
@@ -184,66 +195,79 @@
             preferred_element_type=jnp.float32,
         )
 
-    for phase in range(2):
-        side = side_of(phase)
-        prepare(side)
-        sent_sector = c if phase == 0 else other
-
-        def send_step(chunk, carry):
-            for b in range(CHUNK):
-                w = chunk * CHUNK + b
-                send[phase, w] = partial_sum(side, sent_sector, w).astype(jnp.bfloat16)
-            part_copy(phase, chunk).start()
-            return carry
-
-        lax.fori_loop(0, chunks, send_step, 0)
-
-    for phase in range(2):
-        side = side_of(phase)
-        kept_sector = other if phase == 0 else c
-
-        def keep_step(w, carry):
-            keep[phase, w] = partial_sum(side, kept_sector, w)
-            return carry
-
-        lax.fori_loop(0, columns, keep_step, 0)
-
-        def add_step(chunk, carry):
-            part_copy(phase, chunk).wait_recv()
-            for b in range(CHUNK):
-                w = chunk * CHUNK + b
-                total = keep[phase, w] + recv[phase, w].astype(jnp.float32)
-                final[phase, w] = total.astype(jnp.bfloat16)
-            copy = out_copy(phase, chunk, side)
-            if phase == 0:
-
-                @pl.when(jnp.logical_not(edge))
-                def _():
-                    copy.start()
-
-            else:
-                copy.start()
-            return carry
-
-        lax.fori_loop(0, chunks, add_step, 0)
-
+    far_side, mate_side = side_of(0), side_of(1)
+
+    def send_chunk(phase, chunk):
+        for b in range(CHUNK):
+            w = chunk * CHUNK + b
+            sector = c if phase == 0 else other
+            send[phase, w] = partial_sum(side_of(phase), sector, w).astype(jnp.bfloat16)
+        part_copy(phase, chunk).start()
+
+    def far_send_step(chunk, carry):
+        send_chunk(0, chunk)
+        return carry
+
+    def far_keep_step(w, carry):
+        keep[w] = partial_sum(far_side, other, w)
+        return carry
+
+    def mate_send_step(chunk, carry):
+        send_chunk(1, chunk)
+        part_copy(0, chunk).wait_recv()
+        for b in range(CHUNK):
+            w = chunk * CHUNK + b
+            final[w] = (keep[w] + recv[0, w].astype(jnp.float32)).astype(jnp.bfloat16)
+
+        @pl.when(inner)
+        def _():
+            out_copy(chunk, far_side).start()
+
+        return carry
+
+    def mate_keep_step(chunk, carry):
+        for b in range(CHUNK):
+            w = chunk * CHUNK + b
+            mate_send[w] = partial_sum(mate_side, c, w).astype(jnp.bfloat16)
+        mate_copy(chunk).start()
+        return carry
+
+    def mate_add_step(chunk, carry):
+        mate_copy(chunk).wait_recv()
+        part_copy(1, chunk).wait_recv()
+        for b in range(CHUNK):
+            w = chunk * CHUNK + b
+            total = mate_recv[w].astype(jnp.float32) + recv[1, w].astype(jnp.float32)
+            out[far_side, w] = total.astype(jnp.bfloat16)
+        return carry
+
+    def drain_step(chunk, carry):
+        part_copy(0, chunk).wait_send()
+        part_copy(1, chunk).wait_send()
+        mate_copy(chunk).wait_send()
+
+        @pl.when(inner)
+        def _():
+            out_copy(chunk, mate_side).wait()
+
+        return carry
+
+    prepare(far_side, c)
+    prepare(mate_side, c)
+    site_copy(far_side, other).wait_recv()
+    prepare(far_side, other)
+    fill_half(far_side)
+    lax.fori_loop(0, chunks, far_send_step, 0)
+    lax.fori_loop(0, columns, far_keep_step, 0)
+    site_copy(mate_side, other).wait_recv()
+    prepare(mate_side, other)
+    fill_half(mate_side)
+    lax.fori_loop(0, chunks, mate_send_step, 0)
+    lax.fori_loop(0, chunks, mate_keep_step, 0)
+    lax.fori_loop(0, chunks, mate_add_step, 0)
     for phase in range(2):
         site_copy(side_of(phase), c).wait_send()
-
-        def drain_step(chunk, carry):
-            part_copy(phase, chunk).wait_send()
-            copy = out_copy(phase, chunk, 1 - side_of(phase))
-            if phase == 0:
-
-                @pl.when(jnp.logical_not(edge))
-                def _():
-                    copy.wait()
-
-            else:
-                copy.wait()
-            return carry
-
-        lax.fori_loop(0, chunks, drain_step, 0)
+    lax.fori_loop(0, chunks, drain_step, 0)
 
     @pl.when(edge)
     def _():
@@ -263,7 +287,7 @@
         functools.partial(kernel, sites),
         out_shape=jax.ShapeDtypeStruct((2,) + blocks, bf16),
         in_specs=[pl.BlockSpec(memory_space=pltpu.HBM)] * len(args),
-        out_specs=pl.BlockSpec(memory_space=pl.ANY),
+        out_specs=pl.BlockSpec(memory_space=pltpu.VMEM),
         scratch_shapes=[
             pltpu.VMEM((2,) + blocks, bf16),
             pltpu.VMEM((2, 2, degree, width, width), bf16),
@@ -275,16 +299,20 @@
             pltpu.VMEM((2, 2 * degree, width, width), f32),
             pltpu.VMEM((2, columns * degree, width, width), bf16),
             pltpu.VMEM((2,) + blocks, bf16),
-            pltpu.VMEM((2,) + blocks, f32),
+            pltpu.VMEM(blocks, f32),
             pltpu.VMEM((2,) + blocks, bf16),
-            pltpu.VMEM((2,) + blocks, bf16),
+            pltpu.VMEM(blocks, bf16),
+            pltpu.VMEM(blocks, bf16),
+            pltpu.VMEM(blocks, bf16),
             pltpu.SemaphoreType.DMA((len(args),)),
             pltpu.SemaphoreType.DMA((2,)),
             pltpu.SemaphoreType.DMA((2,)),
             pltpu.SemaphoreType.DMA((2, chunks)),
             pltpu.SemaphoreType.DMA((2, chunks)),
-            pltpu.SemaphoreType.DMA((2, chunks)),
-            pltpu.SemaphoreType.DMA((2, chunks)),
+            pltpu.SemaphoreType.DMA((chunks,)),
+            pltpu.SemaphoreType.DMA((chunks,)),
+            pltpu.SemaphoreType.DMA((chunks,)),
+            pltpu.SemaphoreType.DMA((chunks,)),
             pltpu.SemaphoreType.DMA,
         ],
         compiler_params=pltpu.CompilerParams(

time: 62.6 us -> 57.5 us (0.919)
  Pallas kernels: 60.3 us -> 55.2 us
    pallas_call x1, Pallas kernels: 60.3 us -> 55.2 us  [on_device(): pl.pallas_call(functools.partial(kernel, sites), out_shape=jax.ShapeDtype...]
where the time goes in v3:
time: 57.5 us; the launch traced here: 57.4 us
  Pallas kernels  55.2 us (96%)
  local copies, waits for them, and re-layouts  1.5 us (3%)
  between operations  0.64 us (1%)
    pallas_call x1, Pallas kernels, on_device(): pl.pallas_call(functools.partial(kernel, sites), out_shape=jax.ShapeDtype...  55.2 us
    another operation x1, local copies, waits for them, and re-layouts, on_device(): return (out[0][None, None], out[1][None, None])  1.5 us

profile of v3, /device:TPU:1, one launch (start us, length us, event | category | flops | bytes accessed | tf_op | source)
XLA Modules:
  0.0 57.4 jit_solution(6641767347291378443)
XLA Ops:
  0.6 55.2 %shard_map.131 = bf16[2,30,128,128]{3,2,1,0:T(8,128)(2,1)S(1)} custom-call(bf16[1,1,30,128,128]{4,3,2,1,0:T(8,128)(2,1)} %left_env.1, bf16[1,1,30,128,128]{4,3,2,1,0:T(8,128)(2,1)} %right_env.1, bf16[1,1,4,128,128]{4,3,2,1,0:T(8,128)(2,1)} %left_site.1, bf16[1,1,4,128,128]{4,3,2,1,0:T(8,128)(2,1)} %right_site.1, s32[1,2,30]{2,1,0:T(2,128)} %left_ket.1, ...), custom_call_target="tpu_custom_call" | custom-call | tf_op jit(solution)/shard_map/pallas_call | solution.py:286
  55.9 1.5 %slice_bitcast_fusion = (bf16[1,1,30,128,128]{4,3,2,1,0:T(8,128)(2,1)}, bf16[1,1,30,128,128]{4,3,2,1,0:T(8,128)(2,1)}) fusion(bf16[2,30,128,128]{3,2,1,0:T(8,128)(2,1)S(1)} %shard_map.131), kind=kLoop, calls=%fused_computation | loop fusion | bytes 3932160 | tf_op jit(solution)/shard_map/broadcast_in_dim;squeeze | solution.py:322

commit v4 on v3

--- a/solution.py
+++ b/solution.py
@@ -8,7 +8,7 @@
 from jax.sharding import PartitionSpec as P
 
 MESH = pl.DeviceIdType.MESH
-CHUNK = 2
+CHUNK = 5
 HALF_STEP = 10
 
 
@@ -75,26 +75,25 @@
         site_in, env_in, sizes_in, ket_in, terms_in, weight_in = refs
         for source, target in (
             (site_in.at[0, 0], site.at[side, c]),
+            (sizes_in.at[0], sizes.at[side]),
             (env_in.at[0, 0], env.at[side]),
-            (sizes_in.at[0], sizes.at[side]),
             (ket_in.at[0], ket.at[side]),
             (terms_in.at[0], terms.at[side]),
             (weight_in.at[0], weight.at[side]),
         ):
             loads.append(pltpu.make_async_copy(source, target, load_sem.at[len(loads)]))
-    for load in loads:
-        load.start()
-
+    far_count = jnp.where(inner, 1, 0)
     barrier = pltpu.get_barrier_semaphore()
-    for peer in ((g, other), (mate, c), (mate, other)):
+
+    def greet(peer):
         pl.semaphore_signal(barrier, inc=1, device_id=peer, device_id_type=MESH)
 
-    @pl.when(inner)
-    def _():
-        pl.semaphore_signal(barrier, inc=1, device_id=(far, other), device_id_type=MESH)
-
-    pl.semaphore_wait(barrier, jnp.where(inner, 4, 3))
+    greet((g, other))
     per_side = len(loads) // 2
+    for i in range(per_side):
+        loads[i].start()
+        loads[per_side + i].start()
+    pl.semaphore_wait(barrier, jnp.where(core == 1, 1, 3 + far_count))
     loads[0].wait()
     loads[per_side].wait()
 
@@ -140,14 +139,21 @@
 
     for phase in range(2):
         site_copy(side_of(phase), c).start()
-    for side in range(2):
-        for load in loads[side * per_side + 1 : (side + 1) * per_side]:
-            load.wait()
+    greet((mate, c))
+    greet((mate, other))
+
+    @pl.when(inner)
+    def _():
+        greet((far, other))
+
+
+    def await_loads(first, last):
+        for i in range(first, last):
+            loads[i].wait()
+            loads[per_side + i].wait()
+
+    await_loads(1, 2)
     edge_copy = pltpu.make_async_copy(env.at[core], out.at[core], edge_sem)
-
-    @pl.when(edge)
-    def _():
-        edge_copy.start()
 
     row = lax.broadcasted_iota(jnp.int32, (width, width), 0)
 
@@ -233,46 +239,52 @@
         return carry
 
     def mate_add_step(chunk, carry):
-        mate_copy(chunk).wait_recv()
-        part_copy(1, chunk).wait_recv()
+        mate_copy(chunk).wait()
+        part_copy(0, chunk).wait_send()
+
+        @pl.when(inner)
+        def _():
+            out_copy(chunk, mate_side).wait()
+
+        part_copy(1, chunk).wait()
         for b in range(CHUNK):
             w = chunk * CHUNK + b
             total = mate_recv[w].astype(jnp.float32) + recv[1, w].astype(jnp.float32)
             out[far_side, w] = total.astype(jnp.bfloat16)
         return carry
 
-    def drain_step(chunk, carry):
-        part_copy(0, chunk).wait_send()
-        part_copy(1, chunk).wait_send()
-        mate_copy(chunk).wait_send()
-
-        @pl.when(inner)
-        def _():
-            out_copy(chunk, mate_side).wait()
-
-        return carry
-
     prepare(far_side, c)
     prepare(mate_side, c)
+    await_loads(2, 4)
     site_copy(far_side, other).wait_recv()
     prepare(far_side, other)
     fill_half(far_side)
+    await_loads(4, per_side)
     lax.fori_loop(0, chunks, far_send_step, 0)
+
+    @pl.when(edge)
+    def _():
+        edge_copy.start()
+
     lax.fori_loop(0, columns, far_keep_step, 0)
     site_copy(mate_side, other).wait_recv()
     prepare(mate_side, other)
     fill_half(mate_side)
+
+    @pl.when(core == 1)
+    def _():
+        pl.semaphore_wait(barrier, 2 + far_count)
+
     lax.fori_loop(0, chunks, mate_send_step, 0)
     lax.fori_loop(0, chunks, mate_keep_step, 0)
-    lax.fori_loop(0, chunks, mate_add_step, 0)
-    for phase in range(2):
-        site_copy(side_of(phase), c).wait_send()
-    lax.fori_loop(0, chunks, drain_step, 0)
 
     @pl.when(edge)
     def _():
         edge_copy.wait()
 
+    for phase in range(2):
+        site_copy(side_of(phase), c).wait_send()
+    lax.fori_loop(0, chunks, mate_add_step, 0)
 
 def on_device(*args):
     args = args[:6] + tuple(jnp.swapaxes(table, -1, -2) for table in args[6:10]) + args[10:]

time: 57.5 us -> 55.9 us (0.972)
  the two profiles are of different devices: /device:TPU:1 before, /device:TPU:195 now
where the time goes in v4:
time: 55.9 us; the launch traced here: 55.8 us
  Pallas kernels  53.7 us (96%)
  local copies, waits for them, and re-layouts  1.5 us (3%)
  between operations  0.64 us (1%)
    pallas_call x1, Pallas kernels, on_device(): pl.pallas_call(functools.partial(kernel, sites), out_shape=jax.ShapeDtype...  53.7 us
    another operation x1, local copies, waits for them, and re-layouts, on_device(): return (out[0][None, None], out[1][None, None])  1.5 us

profile of v4, /device:TPU:195, one launch (start us, length us, event | category | flops | bytes accessed | tf_op | source)
XLA Modules:
  0.0 55.8 jit_solution(11838879959424920734)
XLA Ops:
  0.6 53.7 %shard_map.131 = bf16[2,30,128,128]{3,2,1,0:T(8,128)(2,1)S(1)} custom-call(bf16[1,1,30,128,128]{4,3,2,1,0:T(8,128)(2,1)} %left_env.1, bf16[1,1,30,128,128]{4,3,2,1,0:T(8,128)(2,1)} %right_env.1, bf16[1,1,4,128,128]{4,3,2,1,0:T(8,128)(2,1)} %left_site.1, bf16[1,1,4,128,128]{4,3,2,1,0:T(8,128)(2,1)} %right_site.1, s32[1,2,30]{2,1,0:T(2,128)} %left_ket.1, ...), custom_call_target="tpu_custom_call" | custom-call | tf_op jit(solution)/shard_map/pallas_call | solution.py:298
  54.3 1.5 %slice_bitcast_fusion = (bf16[1,1,30,128,128]{4,3,2,1,0:T(8,128)(2,1)}, bf16[1,1,30,128,128]{4,3,2,1,0:T(8,128)(2,1)}) fusion(bf16[2,30,128,128]{3,2,1,0:T(8,128)(2,1)S(1)} %shard_map.131), kind=kLoop, calls=%fused_computation | loop fusion | bytes 3932160 | tf_op jit(solution)/shard_map/broadcast_in_dim;squeeze | solution.py:334

commit v5 on v4

--- a/solution.py
+++ b/solution.py
@@ -52,6 +52,7 @@
     out_send_sem,
     out_recv_sem,
     edge_sem,
+    answer_sem,
 ):
     columns, width = env.shape[1], env.shape[2]
     degree = site.shape[2]
@@ -85,10 +86,20 @@
     far_count = jnp.where(inner, 1, 0)
     barrier = pltpu.get_barrier_semaphore()
 
-    def greet(peer):
-        pl.semaphore_signal(barrier, inc=1, device_id=peer, device_id_type=MESH)
-
-    greet((g, other))
+    def greet(sem):
+        @pl.when(inner)
+        def _():
+            pl.semaphore_signal(sem, inc=1, device_id=(far, other), device_id_type=MESH)
+
+        for peer in ((mate, c), (mate, other)):
+            pl.semaphore_signal(sem, inc=1, device_id=peer, device_id_type=MESH)
+
+    pl.semaphore_signal(barrier, inc=1, device_id=(g, other), device_id_type=MESH)
+
+    @pl.when(core == 1)
+    def _():
+        greet(barrier)
+
     per_side = len(loads) // 2
     for i in range(per_side):
         loads[i].start()
@@ -139,12 +150,10 @@
 
     for phase in range(2):
         site_copy(side_of(phase), c).start()
-    greet((mate, c))
-    greet((mate, other))
-
-    @pl.when(inner)
-    def _():
-        greet((far, other))
+
+    @pl.when(core == 0)
+    def _():
+        greet(answer_sem)
 
 
     def await_loads(first, last):
@@ -273,7 +282,7 @@
 
     @pl.when(core == 1)
     def _():
-        pl.semaphore_wait(barrier, 2 + far_count)
+        pl.semaphore_wait(answer_sem, 2 + far_count)
 
     lax.fori_loop(0, chunks, mate_send_step, 0)
     lax.fori_loop(0, chunks, mate_keep_step, 0)
@@ -326,6 +335,7 @@
             pltpu.SemaphoreType.DMA((chunks,)),
             pltpu.SemaphoreType.DMA((chunks,)),
             pltpu.SemaphoreType.DMA,
+            pltpu.SemaphoreType.REGULAR,
         ],
         compiler_params=pltpu.CompilerParams(
             collective_id=0, has_side_effects=True, vmem_limit_bytes=40 * 1024 * 1024

time: 55.9 us -> 55.1 us (0.986)
  the two profiles are of different devices: /device:TPU:195 before, /device:TPU:1 now
where the time goes in v5:
time: 55.1 us; the launch traced here: 54.7 us
  Pallas kernels  52.5 us (95%)
  local copies, waits for them, and re-layouts  1.5 us (3%)
  between operations  0.64 us (1%)
    pallas_call x1, Pallas kernels, on_device(): pl.pallas_call(functools.partial(kernel, sites), out_shape=jax.ShapeDtype...  52.5 us
    another operation x1, local copies, waits for them, and re-layouts, on_device(): return (out[0][None, None], out[1][None, None])  1.5 us

profile of v5, /device:TPU:1, one launch (start us, length us, event | category | flops | bytes accessed | tf_op | source)
XLA Modules:
  0.0 54.7 jit_solution(9686714163661264696)
XLA Ops:
  0.6 52.5 %shard_map.131 = bf16[2,30,128,128]{3,2,1,0:T(8,128)(2,1)S(1)} custom-call(bf16[1,1,30,128,128]{4,3,2,1,0:T(8,128)(2,1)} %left_env.1, bf16[1,1,30,128,128]{4,3,2,1,0:T(8,128)(2,1)} %right_env.1, bf16[1,1,4,128,128]{4,3,2,1,0:T(8,128)(2,1)} %left_site.1, bf16[1,1,4,128,128]{4,3,2,1,0:T(8,128)(2,1)} %right_site.1, s32[1,2,30]{2,1,0:T(2,128)} %left_ket.1, ...), custom_call_target="tpu_custom_call" | custom-call | tf_op jit(solution)/shard_map/pallas_call | solution.py:307
  53.2 1.5 %slice_bitcast_fusion = (bf16[1,1,30,128,128]{4,3,2,1,0:T(8,128)(2,1)}, bf16[1,1,30,128,128]{4,3,2,1,0:T(8,128)(2,1)}) fusion(bf16[2,30,128,128]{3,2,1,0:T(8,128)(2,1)S(1)} %shard_map.131), kind=kLoop, calls=%fused_computation | loop fusion | bytes 3932160 | tf_op jit(solution)/shard_map/broadcast_in_dim;squeeze | solution.py:344

commit v6 on v5

--- a/solution.py
+++ b/solution.py
@@ -8,8 +8,8 @@
 from jax.sharding import PartitionSpec as P
 
 MESH = pl.DeviceIdType.MESH
-CHUNK = 5
-HALF_STEP = 10
+HEAD, CHUNK, TAIL = (2,), 6, (4,)
+HALF_STEP = 15
 
 
 def kernel(
@@ -57,7 +57,7 @@
     columns, width = env.shape[1], env.shape[2]
     degree = site.shape[2]
     term_count = terms.shape[3] // 2
-    chunks = columns // CHUNK
+    middle = (columns - sum(HEAD) - sum(TAIL)) // CHUNK
     g, c = lax.axis_index("site"), lax.axis_index("sector")
     core = lax.rem(g, 2)
     other = 1 - c
@@ -121,13 +121,30 @@
             device_id_type=MESH,
         )
 
+    def each_chunk(step):
+        first = 0
+        for i, size in enumerate(HEAD):
+            step(i, first, size)
+            first += size
+
+        def one(i, carry):
+            step(len(HEAD) + i, first + i * CHUNK, CHUNK)
+            return carry
+
+        lax.fori_loop(0, middle, one, 0)
+        last = first + middle * CHUNK
+        for i, size in enumerate(TAIL):
+            step(len(HEAD) + middle + i, last, size)
+            last += size
+
     def chunk_copy(source, target, send_sems, recv_sems, chunk, device):
-        blocks = pl.ds(chunk * CHUNK, CHUNK)
+        index, first, size = chunk
+        blocks = pl.ds(first, size)
         return pltpu.make_async_remote_copy(
             src_ref=source.at[blocks],
             dst_ref=target.at[blocks],
-            send_sem=send_sems.at[chunk],
-            recv_sem=recv_sems.at[chunk],
+            send_sem=send_sems.at[index],
+            recv_sem=recv_sems.at[index],
             device_id=device,
             device_id_type=MESH,
         )
@@ -213,41 +230,37 @@
     far_side, mate_side = side_of(0), side_of(1)
 
     def send_chunk(phase, chunk):
-        for b in range(CHUNK):
-            w = chunk * CHUNK + b
+        for b in range(chunk[2]):
+            w = chunk[1] + b
             sector = c if phase == 0 else other
             send[phase, w] = partial_sum(side_of(phase), sector, w).astype(jnp.bfloat16)
         part_copy(phase, chunk).start()
 
-    def far_send_step(chunk, carry):
+    def far_send_step(*chunk):
         send_chunk(0, chunk)
-        return carry
 
     def far_keep_step(w, carry):
         keep[w] = partial_sum(far_side, other, w)
         return carry
 
-    def mate_send_step(chunk, carry):
+    def mate_send_step(*chunk):
         send_chunk(1, chunk)
         part_copy(0, chunk).wait_recv()
-        for b in range(CHUNK):
-            w = chunk * CHUNK + b
+        for b in range(chunk[2]):
+            w = chunk[1] + b
             final[w] = (keep[w] + recv[0, w].astype(jnp.float32)).astype(jnp.bfloat16)
 
         @pl.when(inner)
         def _():
             out_copy(chunk, far_side).start()
 
-        return carry
-
-    def mate_keep_step(chunk, carry):
-        for b in range(CHUNK):
-            w = chunk * CHUNK + b
+    def mate_keep_step(*chunk):
+        for b in range(chunk[2]):
+            w = chunk[1] + b
             mate_send[w] = partial_sum(mate_side, c, w).astype(jnp.bfloat16)
         mate_copy(chunk).start()
-        return carry
-
-    def mate_add_step(chunk, carry):
+
+    def mate_add_step(*chunk):
         mate_copy(chunk).wait()
         part_copy(0, chunk).wait_send()
 
@@ -256,11 +269,10 @@
             out_copy(chunk, mate_side).wait()
 
         part_copy(1, chunk).wait()
-        for b in range(CHUNK):
-            w = chunk * CHUNK + b
+        for b in range(chunk[2]):
+            w = chunk[1] + b
             total = mate_recv[w].astype(jnp.float32) + recv[1, w].astype(jnp.float32)
             out[far_side, w] = total.astype(jnp.bfloat16)
-        return carry
 
     prepare(far_side, c)
     prepare(mate_side, c)
@@ -269,7 +281,7 @@
     prepare(far_side, other)
     fill_half(far_side)
     await_loads(4, per_side)
-    lax.fori_loop(0, chunks, far_send_step, 0)
+    each_chunk(far_send_step)
 
     @pl.when(edge)
     def _():
@@ -284,8 +296,8 @@
     def _():
         pl.semaphore_wait(answer_sem, 2 + far_count)
 
-    lax.fori_loop(0, chunks, mate_send_step, 0)
-    lax.fori_loop(0, chunks, mate_keep_step, 0)
+    each_chunk(mate_send_step)
+    each_chunk(mate_keep_step)
 
     @pl.when(edge)
     def _():
@@ -293,14 +305,14 @@
 
     for phase in range(2):
         site_copy(side_of(phase), c).wait_send()
-    lax.fori_loop(0, chunks, mate_add_step, 0)
+    each_chunk(mate_add_step)
 
 def on_device(*args):
     args = args[:6] + tuple(jnp.swapaxes(table, -1, -2) for table in args[6:10]) + args[10:]
     left_env, left_site, left_ket, left_terms = args[0], args[2], args[4], args[6]
     columns, width = left_env.shape[2], left_env.shape[3]
     degree = left_site.shape[2]
-    chunks = columns // CHUNK
+    chunks = len(HEAD) + (columns - sum(HEAD) - sum(TAIL)) // CHUNK + len(TAIL)
     blocks = (columns, width, width)
     bf16, f32 = jnp.bfloat16, jnp.float32
     sites = lax.axis_size("site")

time: 55.1 us -> 55.1 us (level)
  no operation moved by 1% of the time
where the time goes in v6:
time: 55.1 us; the launch traced here: 54.6 us
  Pallas kernels  52.5 us (95%)
  local copies, waits for them, and re-layouts  1.5 us (3%)
  between operations  0.64 us (1%)
    pallas_call x1, Pallas kernels, on_device(): pl.pallas_call(functools.partial(kernel, sites), out_shape=jax.ShapeDtype...  52.5 us
    another operation x1, local copies, waits for them, and re-layouts, on_device(): return (out[0][None, None], out[1][None, None])  1.5 us

profile of v6, /device:TPU:1, one launch (start us, length us, event | category | flops | bytes accessed | tf_op | source)
XLA Modules:
  0.0 54.6 jit_solution(6172560002684702668)
XLA Ops:
  0.6 52.5 %shard_map.131 = bf16[2,30,128,128]{3,2,1,0:T(8,128)(2,1)S(1)} custom-call(bf16[1,1,30,128,128]{4,3,2,1,0:T(8,128)(2,1)} %left_env.1, bf16[1,1,30,128,128]{4,3,2,1,0:T(8,128)(2,1)} %right_env.1, bf16[1,1,4,128,128]{4,3,2,1,0:T(8,128)(2,1)} %left_site.1, bf16[1,1,4,128,128]{4,3,2,1,0:T(8,128)(2,1)} %right_site.1, s32[1,2,30]{2,1,0:T(2,128)} %left_ket.1, ...), custom_call_target="tpu_custom_call" | custom-call | tf_op jit(solution)/shard_map/pallas_call | solution.py:319
  53.2 1.5 %slice_bitcast_fusion = (bf16[1,1,30,128,128]{4,3,2,1,0:T(8,128)(2,1)}, bf16[1,1,30,128,128]{4,3,2,1,0:T(8,128)(2,1)}) fusion(bf16[2,30,128,128]{3,2,1,0:T(8,128)(2,1)S(1)} %shard_map.131), kind=kLoop, calls=%fused_computation | loop fusion | bytes 3932160 | tf_op jit(solution)/shard_map/broadcast_in_dim;squeeze | solution.py:356
